TPU v7x, 128 devices: a whole 4x4x4 slice. The times are simulated.
128 devices in a mesh: rep: 16 (over z_lo, y, core), tp: 8 (over z_hi, x).
Axes of the slice: x: 4, y: 4, z: 4 (z_hi: 2, z_lo: 2; z = z_hi * 2 + z_lo), core: 2. Of those that a mesh axis runs over, the one named last changes fastest.
Arguments:
- tokens: bfloat16 [16384, 4608], P('rep'), may hold values from -5 to 5
- gain_pre: float32 [4608], replicated, may hold values from 0.5 to 1.5
- gain_post: float32 [4608], replicated, may hold values from 0.5 to 1.5
- qkv_shards: bfloat16 [16, 4608, 256], P('rep', 'tp'), may hold values from -0.5 to 0.5
- out_shards: bfloat16 [16, 128, 4608], P('rep', None, 'tp'), may hold values from -0.125 to 0.125
- shard_map: int32 [16], replicated, may hold values from 0 to 15, as said below
- positions: int32 [16384], P('rep'), may hold values from 0 to 1023, as said below
Outputs:
- layer_out: bfloat16 [16384, 4608], P('rep')
Inputs may be any that keep to these rules, and one draw needn't show every extreme that they name: `shard_map`: each of 0 to 15 appears exactly once. Within each aligned block of 1024 tokens the positions start at 0 and each next position is one more than the one before or 0; the first block holds one document.
All inputs are finite; a program needn't handle non-finite values.
Results may differ from a plain program's by a relative error of at most 0.019.
Values may be sent and summed in bfloat16 or wider, within the bound.
A program may use at most 128 MiB of HBM per device.

v0:
```python
import math

import jax
import jax.numpy as jnp
from jax import lax
from jax.sharding import PartitionSpec as P

HEADS = 16
KVH = 8
HDIM = 128


QUERY_SCALE = 1.0 / 12.0
EPS = 1e-06


def rotate(values, positions):
    half_dim = values.shape[-1] // 2
    freq_index = jnp.arange(half_dim, dtype=jnp.float32)
    frequency = jnp.exp(freq_index * (-2.0 * math.log(10000.0) / values.shape[-1]))
    angles = positions.astype(jnp.float32)[:, None] * frequency[None, :]
    shape_out = (values.shape[0],) + (1,) * (values.ndim - 2) + (half_dim,)
    cosine = jnp.cos(angles).reshape(shape_out)
    sine_part = jnp.sin(angles).reshape(shape_out)
    lower_half = values[..., :half_dim]
    upper_half = values[..., half_dim:]
    return jnp.concatenate(
        [
            lower_half * cosine - upper_half * sine_part,
            upper_half * cosine + lower_half * sine_part,
        ],
        axis=-1,
    )


def attend(projected, positions):
    row_count = projected.shape[0]
    per_group = HEADS // KVH
    groups = projected.reshape(row_count, -1, (per_group + 2) * HDIM)
    queries = groups[:, :, : per_group * HDIM].reshape(row_count, -1, per_group, HDIM)
    key_rows = groups[:, :, per_group * HDIM : (per_group + 1) * HDIM]
    value_rows = groups[:, :, (per_group + 1) * HDIM :]
    queries = (rotate(queries, positions) * QUERY_SCALE).astype(jnp.bfloat16)
    key_rows = rotate(key_rows, positions).astype(jnp.bfloat16)
    value_rows = value_rows.astype(jnp.bfloat16)
    scores = jnp.einsum("tgqd,sgd->gqts", queries, key_rows, preferred_element_type=jnp.float32)
    row_index = jnp.arange(row_count, dtype=jnp.int32)
    allowed = (row_index[None, :] <= row_index[:, None]) & (
        row_index[None, :] >= row_index[:, None] - positions[:, None]
    )
    scores = jnp.where(allowed, scores, -1e30)
    row_max = jnp.max(scores, axis=-1, keepdims=True)
    powers = jnp.exp(scores - row_max)
    row_total = jnp.sum(powers, axis=-1, keepdims=True)
    attn_weights = (powers / row_total).astype(jnp.bfloat16)
    head_out = jnp.einsum(
        "gqts,sgd->tgqd", attn_weights, value_rows, preferred_element_type=jnp.float32
    )
    return head_out.astype(jnp.bfloat16).reshape(row_count, -1)


def on_device(tokens, gain_pre, gain_post, qkv_shards, out_shards, shard_map, positions):
    rep_count = lax.axis_size("rep")
    tp_count = lax.axis_size("tp")
    per_member = rep_count // tp_count
    order = jnp.arange(rep_count, dtype=jnp.int32)
    inverse = jnp.sum(jnp.where(shard_map[:, None] == order[None, :], order[:, None], 0), axis=0)
    row_count = tokens.shape[0]
    stream = tokens.astype(jnp.float32)
    mean_square = jnp.mean(stream * stream, axis=1, keepdims=True)
    normed = (stream * lax.rsqrt(mean_square + EPS) * gain_pre).astype(jnp.bfloat16)
    blocks = lax.all_gather(qkv_shards, "rep", axis=0, tiled=True)
    blocks = jnp.take(blocks, inverse, axis=0)
    blocks = blocks.reshape(tp_count, per_member, blocks.shape[1], blocks.shape[2])
    local_qkv = lax.all_to_all(blocks, "tp", split_axis=0, concat_axis=2, tiled=True)
    projected = jnp.einsum("td,pdc->tpc", normed, local_qkv[0], preferred_element_type=jnp.float32)
    projected = projected.reshape(row_count, -1)
    head_out = attend(projected, positions)
    head_parts = head_out.reshape(row_count, per_member, -1)
    out_blocks = lax.all_gather(out_shards, "rep", axis=0, tiled=True)
    out_blocks = jnp.take(out_blocks, inverse, axis=0)
    out_blocks = out_blocks.reshape(tp_count, per_member, out_blocks.shape[1], out_blocks.shape[2])
    local_out = lax.all_to_all(out_blocks, "tp", split_axis=0, concat_axis=3, tiled=True)
    partial_sum = jnp.einsum(
        "tpr,prd->td", head_parts, local_out[0], preferred_element_type=jnp.float32
    )
    summed = lax.psum(partial_sum.astype(jnp.bfloat16), "tp").astype(jnp.float32)
    mean_out = jnp.mean(summed * summed, axis=1, keepdims=True)
    return (stream + summed * lax.rsqrt(mean_out + EPS) * gain_post).astype(jnp.bfloat16)


def solution(mesh):
    placed = (P("rep", None), P(), P(), P("rep", "tp", None), P("rep", None, "tp"), P(), P("rep"))
    return jax.shard_map(
        on_device, mesh=mesh, in_specs=placed, out_specs=P("rep", None), check_vma=False
    )
```

profile of v0, /device:TPU:1, one launch (start us, length us, event | category | flops | bytes accessed | tf_op | source)
XLA Modules:
  0.0 473.2 jit_solution(4951800961561932497)
XLA Ops:
  6.5 0.0 all-gather.5.cloned.1.call-start
  6.5 0.7 all-gather.5.cloned.1.call-update
  7.3 0.0 all-gather.3.cloned.1.call-start
  7.3 0.7 all-gather.3.cloned.1.call-update
  8.0 0.7 select_reduce_fusion
  8.7 0.1 reduce_sum.42
  8.9 38.3 %all-gather.5.cloned.1.call-done = bf16[16,128,576]{1,2,0:T(8,128)(2,1)} async-done(((bf16[1,128,576]{1,2,0:T(8,128)(2,1)}), bf16[16,128,576]{1,2,0:T(8,128)(2,1)}) %all-gather.5.cloned.1.call-update) | async-done | bytes 2359312 | tf_op jit(solution)/shard_map/all_gather | solution.py:80
  47.2 2.7 gather_fusion.1
  49.8 1.7 broadcast_select_fusion.1
  51.6 6.3 %all-to-all-start.1 = ((bf16[8,2,128,576]{2,3,1,0:T(8,128)(2,1)}), bf16[8,2,128,576]{2,3,1,0:T(8,128)(2,1)S(1)}, u32[]{:S(2)}, u32[]{:S(2)}) async-start(bf16[8,2,128,576]{2,3,1,0:T(8,128)(2,1)} %broadcast_select_fusion.1), calls=%async_computation.1 | async-start | bytes 4718592 | tf_op jit(solution)/shard_map/all_to_all | solution.py:83
  57.9 53.4 %all-gather.3.cloned.1.call-done = bf16[16,576,256]{2,1,0:T(8,128)(2,1)} async-done(((bf16[1,576,256]{2,1,0:T(8,128)(2,1)}), bf16[16,576,256]{2,1,0:T(8,128)(2,1)}) %all-gather.3.cloned.1.call-update) | async-done | bytes 4718608 | tf_op jit(solution)/shard_map/all_gather | solution.py:72
  111.2 5.4 %gather_fusion = bf16[16,576,256]{2,1,0:T(8,128)(2,1)} fusion(bf16[16,576,256]{2,1,0:T(8,128)(2,1)} %all-gather.3.cloned.1.call-done, s32[1024]{0:T(1024)S(1)} %pad_clamp_fusion), kind=kCustom, calls=%fused_computation | custom fusion | bytes 9437248 | tf_op jit(solution)/shard_map/jit(_take)/gather | solution.py:73
  116.6 5.0 %broadcast_select_fusion = bf16[8,2,576,256]{3,2,1,0:T(8,128)(2,1)} fusion(bf16[8,2,576,256]{3,2,1,0:T(8,128)(2,1)} %bitcast.80, pred[8,2]{1,0:T(8,128)(4,1)S(1)} %compare_and_fusion), kind=kLoop, calls=%fused_computation.22 | loop fusion | flops 2359296 | bytes 9437200 | tf_op jit(solution)/shard_map/jit(_take)/select_n | solution.py:73
  121.6 0.0 copy-start.5
  121.6 0.0 all-to-all-done.1
  121.6 6.6 %all-to-all-start = ((bf16[8,2,576,256]{3,2,1,0:T(8,128)(2,1)}), bf16[8,2,576,256]{3,2,1,0:T(8,128)(2,1)}, u32[]{:S(2)}, u32[]{:S(2)}) async-start(bf16[8,2,576,256]{3,2,1,0:T(8,128)(2,1)} %broadcast_select_fusion), calls=%async_computation | async-start | bytes 9437184 | tf_op jit(solution)/shard_map/all_to_all | solution.py:75
  128.2 0.0 all-reduce.2.cloned.1.call-start
  128.3 5.6 %fusion.2 = f32[1024]{0:T(1024)S(1)} fusion(bf16[1024,4608]{1,0:T(8,128)(2,1)} %param.7), kind=kLoop, calls=%fused_computation.9 | loop fusion | flops 14154752 | bytes 9441280 | tf_op jit(solution)/shard_map/reduce_sum | solution.py:70
  133.9 0.0 copy-done.5
  133.9 3.3 multiply_cosine_fusion
  137.1 0.6 fusion.14
  137.7 1.6 copy.48
  139.3 45.7 %all-to-all-done = bf16[8,2,576,256]{3,2,1,0:T(8,128)(2,1)} async-done(((bf16[8,2,576,256]{3,2,1,0:T(8,128)(2,1)}), bf16[8,2,576,256]{3,2,1,0:T(8,128)(2,1)}, u32[]{:S(2)}, u32[]{:S(2)}) %all-to-all-start) | async-done | bytes 4718624 | tf_op jit(solution)/shard_map/all_to_all | solution.py:75
  185.0 0.0 copy-start.6
  185.0 5.0 %copy.42 = bf16[1,2,8,576,256]{4,3,2,1,0:T(8,128)(2,1)} copy(bf16[1,2,8,576,256]{4,3,1,2,0:T(8,128)(2,1)} %bitcast.4) | data formatting | bytes 9437184 | tf_op jit(solution)/shard_map/all_to_all | solution.py:75
  190.0 6.7 %copy.43 = bf16[2,256,4608]{2,1,0:T(8,128)(2,1)} copy(bf16[2,256,4608]{1,2,0:T(8,128)(2,1)} %bitcast.81) | data formatting | bytes 9437184 | tf_op jit(solution)/shard_map/td,pdc->tpc/dot_general | solution.py:76
  196.7 0.0 copy-done.6
  196.7 9.5 %fusion.15 = f32[1024,1,512]{0,2,1:T(8,128)S(1)} fusion(bf16[512,4608]{1,0:T(8,128)(2,1)} %bitcast.84, bf16[1024,4608]{1,0:T(8,128)(2,1)} %param.7, f32[4608]{0:T(1024)S(1)} %copy-done.6, f32[1024]{0:T(1024)S(1)} %add_rsqrt_fusion.1), kind=kOutput, calls=%fused_computation.29 | convolution fusion | flops 4850712576 | bytes 16275456 | tf_op jit(solution)/shard_map/td,pdc->tpc/dot_general | solution.py:76
  206.2 0.0 copy-start.3
  206.2 1.8 fusion.44
  208.0 0.1 slice.35
  208.1 0.9 fusion.51
  208.9 0.0 copy-done.3
  209.0 0.3 copy.57
  209.3 1.4 copy.56
  210.7 1.4 subtract_bitcast_fusion
  212.1 0.0 copy-start.2
  212.1 2.9 fusion.10
  215.0 0.0 copy-start.1
  215.0 3.2 copy-done.1
  218.2 1.7 fusion.11
  219.9 0.0 copy-done.2
  220.0 10.1 %bitcast_convert_fusion = bf16[1024,4608]{1,0:T(8,128)(2,1)} fusion(bf16[2,128,4608]{1,2,0:T(8,128)(2,1)S(1)} %bitcast.86, f32[2,1024]{1,0:T(2,128)S(1)} %fusion.11, f32[2,1024]{1,0:T(2,128)S(1)} %get-tuple-element.15, f32[1024,1024,2]{1,0,2:T(8,128)} %copy-done.1, pred[1024,1024]{0,1:T(8,128)(4,1)S(1)} %fusion.14, f32[1024,1,512]{0,2,1:T(8,128)} %copy-done.3), kind=kOutput, calls=%fused_computation.13 | convolution fusion | flops 2966159360 | bytes 21512192 | tf_op jit(solution)/shard_map/tpr,prd->td/dot_general | solution.py:84
  230.0 0.0 copy-start.4
  230.0 0.0 all-reduce.2.cloned.1.call-update
  230.1 219.4 %all-reduce.2.cloned.1.call-done = bf16[1024,4608]{1,0:T(8,128)(2,1)} async-done(((bf16[1024,4608]{1,0:T(8,128)(2,1)}), bf16[1024,4608]{1,0:T(8,128)(2,1)}) %all-reduce.2.cloned.1.call-update) | async-done | bytes 9437200 | tf_op jit(solution)/shard_map/psum | solution.py:87
  449.5 0.0 copy-start
  449.5 5.7 %fusion = f32[1024]{0:T(1024)S(1)} fusion(bf16[1024,4608]{1,0:T(8,128)(2,1)} %all-reduce.2.cloned.1.call-done), kind=kLoop, calls=%fused_computation.7 | loop fusion | flops 14154752 | bytes 9441280 | tf_op jit(solution)/shard_map/reduce_sum | solution.py:88
  455.2 0.0 copy-done.4
  455.2 0.6 copy-done
  455.8 10.8 %fusion.5 = bf16[1024,4608]{1,0:T(8,128)(2,1)} fusion(bf16[1024,4608]{1,0:T(8,128)(2,1)S(1)} %copy-done, bf16[1024,4608]{1,0:T(8,128)(2,1)} %param.7, f32[4608]{0:T(1024)S(1)} %copy-done.4, f32[1024]{0:T(1024)S(1)} %add_rsqrt_fusion), kind=kLoop, calls=%fused_computation.12 | loop fusion | flops 28311552 | bytes 28334080 | tf_op jit(solution)/shard_map/convert_element_type | solution.py:89
  (7 shorter events, 0.0 us)
Async XLA Ops:
  6.5 40.6 %all-gather.5.cloned.1.call-start = ((), (), s32[]{:S(2)}) async-start(), calls=%async_computation.3 | async-start | bytes 2506752 | tf_op jit(solution)/shard_map/all_gather | solution.py:80
  7.3 104.0 %all-gather.3.cloned.1.call-start = ((), (), s32[]{:S(2)}) async-start(), calls=%async_computation.2 | async-start | bytes 5013504 | tf_op jit(solution)/shard_map/all_gather | solution.py:72
  51.6 70.1 %all-to-all-start.1 = ((bf16[8,2,128,576]{2,3,1,0:T(8,128)(2,1)}), bf16[8,2,128,576]{2,3,1,0:T(8,128)(2,1)S(1)}, u32[]{:S(2)}, u32[]{:S(2)}) async-start(bf16[8,2,128,576]{2,3,1,0:T(8,128)(2,1)} %broadcast_select_fusion.1), calls=%async_computation.1 | async-start | bytes 4718592 | tf_op jit(solution)/shard_map/all_to_all | solution.py:83
  121.6 12.2 %copy-start.5 = (s32[1024]{0:T(1024)S(1)}, s32[1024]{0:T(1024)}, u32[]{:S(2)}) copy-start(s32[1024]{0:T(1024)} %param.13) | copy-start | bytes 12292
  121.6 63.4 %all-to-all-start = ((bf16[8,2,576,256]{3,2,1,0:T(8,128)(2,1)}), bf16[8,2,576,256]{3,2,1,0:T(8,128)(2,1)}, u32[]{:S(2)}, u32[]{:S(2)}) async-start(bf16[8,2,576,256]{3,2,1,0:T(8,128)(2,1)} %broadcast_select_fusion), calls=%async_computation | async-start | bytes 9437184 | tf_op jit(solution)/shard_map/all_to_all | solution.py:75
  128.2 321.2 %all-reduce.2.cloned.1.call-start = ((), (), s32[]{:S(2)}) async-start(), calls=%async_computation.4 | async-start | bytes 18874368 | tf_op jit(solution)/shard_map/psum | solution.py:87
  185.0 11.7 %copy-start.6 = (f32[4608]{0:T(1024)S(1)}, f32[4608]{0:T(1024)}, u32[]{:S(2)}) copy-start(f32[4608]{0:T(1024)} %param.8) | copy-start | bytes 55300
  206.2 2.8 copy-start.3
  212.1 7.8 %copy-start.2 = (bf16[1,2,128,8,576]{2,4,3,1,0:T(8,128)(2,1)S(1)}, bf16[1,2,128,8,576]{2,4,3,1,0:T(8,128)(2,1)}, u32[]{:S(2)}) copy-start(bf16[1,2,128,8,576]{2,4,3,1,0:T(8,128)(2,1)} %copy.48) | copy-start | bytes 7077892
  215.0 3.2 copy-start.1
  230.0 225.2 %copy-start.4 = (f32[4608]{0:T(1024)S(1)}, f32[4608]{0:T(1024)}, u32[]{:S(2)}) copy-start(f32[4608]{0:T(1024)} %param.9) | copy-start | bytes 55300
  449.5 6.4 %copy-start = (bf16[1024,4608]{1,0:T(8,128)(2,1)S(1)}, bf16[1024,4608]{1,0:T(8,128)(2,1)}, u32[]{:S(2)}) copy-start(bf16[1024,4608]{1,0:T(8,128)(2,1)} %all-reduce.2.cloned.1.call-done) | copy-start | bytes 28311556
Sparse Core Ops, SparseCore 0:
  9.1 38.0 all-gather.4
  48.9 62.3 all-gather.2
  230.2 219.2 all-reduce.1
where the time goes:
time: 474 us; the launch traced here: 473 us
  waiting for transfers between devices  358 us (76%)
  other arithmetic  38.4 us (8%)
  local copies, waits for them, and re-layouts  27.9 us (6%)
  matrix products  22.5 us (5%)
  between operations  13.2 us (3%)
  starting transfers between devices  12.9 us (3%)
    psum x1, waiting for transfers between devices, on_device(): lax.psum(partial_sum.astype(jnp.bfloat16), 'tp').astype(jnp.float32)  219 us
    all_gather x1, waiting for transfers between devices, on_device(): blocks = lax.all_gather(qkv_shards, 'rep', axis=0, tiled=True)  53.4 us
    all_to_all x1, waiting for transfers between devices, on_device(): lax.all_to_all(blocks, 'tp', split_axis=0, concat_axis=2, tiled=True)  45.7 us
    all_gather x1, waiting for transfers between devices, on_device(): out_blocks = lax.all_gather(out_shards, 'rep', axis=0, tiled=True)  38.3 us
    convert_element_type x1, other arithmetic, on_device(): (stream + summed * lax.rsqrt(mean_out + EPS) * gain_post).astype(jnp.bflo...  10.8 us
    dot_general x1, matrix products, on_device(): jnp.einsum('tpr,prd->td', head_parts, local_out[0], preferred_element_typ...  10.1 us
    dot_general x1, matrix products, on_device(): jnp.einsum('td,pdc->tpc', normed, local_qkv[0], preferred_element_type=jn...  9.51 us
  transfers between devices with their start and end apart: 5, of which 4 were waited for; matrix products, arithmetic and copies ran while one was open for 6% of the time, Pallas kernels for 0%

commit v1 on v0

v1 whole, which is shorter than its diff:
```python
import math

import jax
import jax.numpy as jnp
import numpy as np
from jax import lax
from jax.experimental import pallas as pl
from jax.experimental.pallas import tpu as pltpu
from jax.sharding import PartitionSpec as P

D = 4608
TOK = 1024
HDIM = 128
CHUNK = 256
N_CHUNK = TOK // CHUNK
SEG = 576
PART = 144
QUERY_SCALE = 1.0 / 12.0
EPS = 1e-06
MESH = pl.DeviceIdType.MESH
F32 = jnp.float32
BF16 = jnp.bfloat16
NT = (((1,), (1,)), ((), ()))
W_ROWS = ((0, 192), (192, 192), (384, 192))
W_ORDER = ("xzy", "yzx", "xyz")


def device(x, y, z, c):
    return ((z % 2) * 8 + y * 2 + c, (z // 2) * 4 + x)


def kernel(
    tok, gpre, gpost, freq, qkv, outs, smap, pos, o_hbm,
    s1, send2, wq, w, h0, h1, h2, h3, normed, qb, kb, vb, cosb, sinb, startb, lhs, att, stream, result,
    s1_ss, s1_rs, s2_ss, s2_rs, s3_ss, s3_rs, w_ss, w_rs, h_ss, h_rs, loc,
):
    hs = (h0, h1, h2, h3)
    rep = lax.axis_index("rep")
    tp = lax.axis_index("tp")
    c, y, zl = rep % 2, (rep // 2) % 4, rep // 8
    x, zh = tp % 4, tp // 4
    z = zh * 2 + zl
    yp, ym, y2 = (y + 1) % 4, (y + 3) % 4, (y + 2) % 4

    def shifted(axis, by):
        at = {"x": x, "y": y, "z": z}
        at[axis] = (at[axis] + by + 4) % 4
        return device(at["x"], at["y"], at["z"], c)

    def remote(src, dst, ss, rs, dev):
        return pltpu.make_async_remote_copy(
            src_ref=src, dst_ref=dst, send_sem=ss, recv_sem=rs, device_id=dev, device_id_type=MESH
        )

    tok_copies = []
    for i in range(N_CHUNK):
        rows = pl.ds(i * CHUNK, CHUNK)
        cp = pltpu.make_async_copy(tok.at[rows], normed.at[rows], loc.at[i])
        cp.start()
        tok_copies.append(cp)

    barrier = pltpu.get_barrier_semaphore()

    def greet_rep(d, _):
        pl.semaphore_signal(barrier, inc=1, device_id=((rep + d) % 16, tp), device_id_type=MESH)
        return 0

    def greet_tp(d, _):
        pl.semaphore_signal(barrier, inc=1, device_id=(rep, (tp + d) % 8), device_id_type=MESH)
        return 0

    lax.fori_loop(1, 16, greet_rep, 0)
    lax.fori_loop(1, 8, greet_tp, 0)
    far = jnp.where(zl == 0, 3, 1)
    pl.semaphore_signal(barrier, inc=1, device_id=device(x, y, (z + far) % 4, c), device_id_type=MESH)
    pl.semaphore_wait(barrier, 23)

    def s1_src(to):
        rows = pl.ds(pl.multiple_of(((to // 2) % 4) * PART, 16), PART)
        cols = pl.ds(pl.multiple_of((to // 8) * 128, 128), 128)
        return qkv.at[0, rows, cols]

    own1 = pltpu.make_async_copy(s1_src(rep), s1.at[rep], loc.at[4])
    own1.start()

    def s1_copy(d):
        to = (rep + d) % 16
        return remote(s1_src(to), s1.at[rep], s1_ss.at[d], s1_rs.at[d], (to, tp))

    def s1_start(d, _):
        s1_copy(d).start()
        return 0

    lax.fori_loop(1, 16, s1_start, 0)

    eye = (
        lax.broadcasted_iota(jnp.int32, (SEG, SEG), 0) == lax.broadcasted_iota(jnp.int32, (SEG, SEG), 1)
    ).astype(BF16)
    w[z, y, c, x] = lax.dot_general(eye, outs[0], NT, preferred_element_type=F32).astype(BF16)

    def w_set(part, step):
        r0, n = W_ROWS[part]
        done = W_ORDER[part][:step]
        at = {"x": x, "y": y, "z": z}
        full = slice(None)
        return w.at[
            full if "z" in done else at["z"],
            full if "y" in done else at["y"],
            c,
            full if "x" in done else at["x"],
            pl.ds(r0, n),
        ]

    w_by = (1, -1, 2)

    def w_copies(part, step):
        axis = W_ORDER[part][step]
        block = w_set(part, step)
        return [
            remote(block, block, w_ss.at[part, step, k], w_rs.at[part, step, k], shifted(axis, by))
            for k, by in enumerate(w_by)
        ]

    def w_start(step):
        for part in range(3):
            for cp in w_copies(part, step):
                cp.start()

    def w_wait(step):
        for part in range(3):
            for cp in w_copies(part, step):
                cp.wait_recv()

    w_start(0)

    lax.fori_loop(1, 16, lambda d, _: (s1_copy(d).wait_recv(), 0)[1], 0)
    own1.wait()

    def order_of(b):
        at = jnp.int32(0)
        for s in range(16):
            at = jnp.where(smap[s] == b, s, at)
        return at

    for t in range(8):
        send2[t] = s1[order_of(2 * t + c)]
    g = c * 2 + zl
    g2 = c * 2 + (1 - zl)

    own2 = pltpu.make_async_copy(send2.at[tp], wq.at[g, tp, y], loc.at[5])
    own2.start()

    def s2_copy(d):
        to = (tp + d) % 8
        return remote(send2.at[to], wq.at[g, tp, y], s2_ss.at[d], s2_rs.at[d], (rep, to))

    lax.fori_loop(1, 8, lambda d, _: (s2_copy(d).start(), 0)[1], 0)

    gain = gpre[...]

    def norm_rows(i, _):
        rows = pl.ds(pl.multiple_of(i * 32, 32), 32)
        v = normed[rows, :].astype(F32)
        ms = jnp.sum(v * v, axis=1, keepdims=True) * (1.0 / D)
        normed[rows, :] = (v * lax.rsqrt(ms + EPS) * gain).astype(BF16)
        return 0

    for cp in tok_copies:
        cp.wait()
    lax.fori_loop(0, TOK // 32, norm_rows, 0)

    w_wait(0)
    w_start(1)

    lax.fori_loop(1, 8, lambda d, _: (s2_copy(d).wait_recv(), 0)[1], 0)
    own2.wait()

    zdev = (((1 - zl) * 8 + y * 2 + c), tp)
    sib = (rep + 1 - 2 * c, tp)
    updev, dndev = shifted("y", 1), shifted("y", -1)
    lo, hi = pl.ds(0, 4), pl.ds(4, 4)
    k3 = [0]
    s3 = []

    def s3_send(block, dev):
        k = k3[0]
        k3[0] += 1
        cp = remote(block, block, s3_ss.at[k], s3_rs.at[k], dev)
        cp.start()
        s3.append(cp)
        return cp

    mine, theirs = wq.at[g, :, y], wq.at[g2, :, y]
    z_cp = s3_send(mine, zdev)
    up_a = s3_send(mine, updev)
    dn_a = s3_send(mine, dndev)
    sibs = [s3_send(mine, sib)]
    pos_t = pos[...].astype(F32).T
    lane = lax.broadcasted_iota(jnp.int32, (128, 128), 1)
    for i in range(8):
        p = pos_t[:, i:i + 1]
        angle = p * freq[...]
        rows = pl.ds(i * 128, 128)
        cosb[rows, :] = jnp.cos(angle)
        sinb[rows, :] = jnp.where(lane < 64, -1.0, 1.0) * jnp.sin(angle)
        row = (lax.broadcasted_iota(jnp.int32, (128, 128), 0) + i * 128)
        startb[rows, :] = row - p.astype(jnp.int32)
    z_cp.wait_recv()
    up_b = s3_send(theirs, updev)
    dn_b = s3_send(theirs, dndev)
    sibs.append(s3_send(theirs, sib))
    up_a.wait_recv()
    f1 = s3_send(wq.at[g, lo, ym], updev)
    sibs.append(s3_send(wq.at[g, :, ym], sib))
    dn_a.wait_recv()
    f2 = s3_send(wq.at[g, hi, yp], dndev)
    sibs.append(s3_send(wq.at[g, :, yp], sib))
    w_wait(1)
    w_start(2)
    up_b.wait_recv()
    f3 = s3_send(wq.at[g2, lo, ym], updev)
    sibs.append(s3_send(wq.at[g2, :, ym], sib))
    dn_b.wait_recv()
    f4 = s3_send(wq.at[g2, hi, yp], dndev)
    sibs.append(s3_send(wq.at[g2, :, yp], sib))
    for f, block in (
        (f1, wq.at[g, lo, y2]), (f2, wq.at[g, hi, y2]), (f3, wq.at[g2, lo, y2]), (f4, wq.at[g2, hi, y2])
    ):
        f.wait_recv()
        sibs.append(s3_send(block, sib))
    for cp in sibs:
        cp.wait_recv()

    def project(i):
        rows = pl.ds(i * CHUNK, CHUNK)
        weights = jnp.concatenate([wq[j].reshape(D, 128) for j in range(4)], axis=1)
        p = jnp.dot(normed[rows, :], weights, preferred_element_type=F32)
        cos, sin = cosb[rows, :], sinb[rows, :]

        def rotate(u):
            return u * cos + pltpu.roll(u, 64, 1) * sin

        for j in range(2):
            qb[j, rows, :] = (rotate(p[:, j * 128:(j + 1) * 128]) * QUERY_SCALE).astype(BF16)
        kb[rows, :] = rotate(p[:, 256:384]).astype(BF16)
        vb[rows, :] = p[:, 384:].astype(BF16)

    def attend(i):
        rows = pl.ds(i * CHUNK, CHUNK)
        n = (i + 1) * CHUNK
        first = startb[rows, 0:1]
        at = lax.broadcasted_iota(jnp.int32, (CHUNK, n), 1)
        row = lax.broadcasted_iota(jnp.int32, (CHUNK, n), 0) + i * CHUNK
        allowed = (at <= row) & (at >= first)
        for j in range(2):
            s = lax.dot_general(qb[j, rows, :], kb[0:n, :], NT, preferred_element_type=F32)
            s = jnp.where(allowed, s, -1e30)
            e = jnp.exp(s - jnp.max(s, axis=1, keepdims=True))
            a = (e * (1.0 / jnp.sum(e, axis=1, keepdims=True))).astype(BF16)
            hs[i][zh, x, j] = jnp.dot(a, vb[0:n, :], preferred_element_type=F32).astype(BF16)

    def h_copy(i, d):
        to = (tp + d) % 8
        block = hs[i].at[zh, x]
        return remote(block, block, h_ss.at[i, d], h_rs.at[i, d], (rep, to))

    for i in range(N_CHUNK):
        project(i)
        attend(i)
        lax.fori_loop(1, 8, lambda d, _: (h_copy(i, d).start(), 0)[1], 0)

    w_wait(2)
    w_sib = []
    for part in range(3):
        r0, n = W_ROWS[part]
        for k in range(2):
            block = w.at[pl.ds(2 * k, 2), :, c, :, pl.ds(r0, n)]
            cp = remote(block, block, w_ss.at[part, 3, k], w_rs.at[part, 3, k], sib)
            cp.start()
            w_sib.append(cp)
    for cp in w_sib:
        cp.wait_recv()

    def out_proj(i):
        rows = pl.ds(i * CHUNK, CHUNK)
        st = pltpu.make_async_copy(tok.at[rows], stream.at[i % 2], loc.at[6 + i % 2])
        st.start()
        for s in range(16):
            b = smap[s]
            lhs[:, s * 128:(s + 1) * 128] = hs[i][b // 8, (b // 2) % 4, b % 2]
        left = lhs[...]
        total = jnp.zeros((CHUNK, 1), F32)
        for half in range(2):
            for k in range(3):
                pieces = []
                n = k * 768
                while n < (k + 1) * 768:
                    xi, r0 = n // SEG, n % SEG
                    r1 = min(SEG, r0 + (k + 1) * 768 - n)
                    pieces.append((xi, r0, r1))
                    n += r1 - r0
                right = jnp.concatenate(
                    [
                        jnp.concatenate(
                            [w[half * 2 + r // 8, (r // 2) % 4, r % 2, xi, r0:r1, :] for xi, r0, r1 in pieces], axis=0
                        )
                        for r in range(16)
                    ],
                    axis=1,
                )
                t = lax.dot_general(left, right, NT, preferred_element_type=F32)
                total = total + jnp.sum(t * t, axis=1, keepdims=True)
                col = half * 2304 + k * 768
                att[:, col:col + 768] = t
        scale = lax.rsqrt(total * (1.0 / D) + EPS)
        st.wait()
        if i >= 2:
            pltpu.make_async_copy(
                result.at[i % 2], o_hbm.at[pl.ds((i - 2) * CHUNK, CHUNK)], loc.at[8 + i % 2]
            ).wait()
        att_scale = scale
        result[i % 2] = (stream[i % 2].astype(F32) + att[...] * att_scale * gpost[...]).astype(BF16)
        pltpu.make_async_copy(result.at[i % 2], o_hbm.at[rows], loc.at[8 + i % 2]).start()

    for i in range(N_CHUNK):
        lax.fori_loop(1, 8, lambda d, _: (h_copy(i, d).wait_recv(), 0)[1], 0)
        out_proj(i)

    lax.fori_loop(1, 16, lambda d, _: (s1_copy(d).wait_send(), 0)[1], 0)
    lax.fori_loop(1, 8, lambda d, _: (s2_copy(d).wait_send(), 0)[1], 0)
    for cp in s3:
        cp.wait_send()
    for step in range(3):
        for part in range(3):
            for cp in w_copies(part, step):
                cp.wait_send()
    for cp in w_sib:
        cp.wait_send()
    for i in range(N_CHUNK):
        lax.fori_loop(1, 8, lambda d, _: (h_copy(i, d).wait_send(), 0)[1], 0)
    for i in (2, 3):
        pltpu.make_async_copy(result.at[i % 2], o_hbm.at[pl.ds(i * CHUNK, CHUNK)], loc.at[8 + i % 2]).wait()


def on_device(tokens, gain_pre, gain_post, qkv_shards, out_shards, shard_map, positions):
    freq = np.exp(np.arange(64) * (-2.0 * math.log(10000.0) / HDIM)).astype(np.float32)
    freq = jnp.asarray(np.concatenate([freq, freq])[None])
    vmem, hbm = pl.BlockSpec(memory_space=pltpu.VMEM), pl.BlockSpec(memory_space=pl.ANY)
    smem = pl.BlockSpec(memory_space=pltpu.SMEM)
    sem = pltpu.SemaphoreType.DMA
    heads = pltpu.VMEM((2, 4, 2, CHUNK, 128), BF16)
    return pl.pallas_call(
        kernel,
        name="attention_block",
        out_shape=jax.ShapeDtypeStruct((TOK, D), BF16),
        in_specs=[hbm, vmem, vmem, vmem, hbm, vmem, smem, vmem],
        out_specs=hbm,
        scratch_shapes=[
            pltpu.VMEM((16, PART, 128), BF16),
            pltpu.VMEM((8, PART, 128), BF16),
            pltpu.VMEM((4, 8, 4, PART, 128), BF16),
            pltpu.VMEM((4, 4, 2, 4, SEG, 128), BF16),
            heads, heads, heads, heads,
            pltpu.VMEM((TOK, D), BF16),
            pltpu.VMEM((2, TOK, 128), BF16),
            pltpu.VMEM((TOK, 128), BF16),
            pltpu.VMEM((TOK, 128), BF16),
            pltpu.VMEM((TOK, 128), F32),
            pltpu.VMEM((TOK, 128), F32),
            pltpu.VMEM((TOK, 128), jnp.int32),
            pltpu.VMEM((CHUNK, 2048), BF16),
            pltpu.VMEM((CHUNK, D), F32),
            pltpu.VMEM((2, CHUNK, D), BF16),
            pltpu.VMEM((2, CHUNK, D), BF16),
            sem((16,)), sem((16,)), sem((8,)), sem((8,)), sem((24,)), sem((24,)),
            sem((3, 4, 3)), sem((3, 4, 3)), sem((4, 8)), sem((4, 8)), sem((10,)),
        ],
        compiler_params=pltpu.CompilerParams(
            collective_id=0, has_side_effects=True, vmem_limit_bytes=62 << 20
        ),
        cost_estimate=pl.CostEstimate(flops=26 * 10**9, bytes_accessed=30 * 10**6, transcendentals=3 * 10**6),
    )(
        tokens, gain_pre.reshape(1, D), gain_post.reshape(1, D), freq, qkv_shards, out_shards, shard_map,
        positions.reshape(8, 128),
    )


def solution(mesh):
    placed = (P("rep", None), P(), P(), P("rep", "tp", None), P("rep", None, "tp"), P(), P("rep"))
    return jax.shard_map(
        on_device, mesh=mesh, in_specs=placed, out_specs=P("rep", None), check_vma=False
    )
```

time: 474 us -> 176 us (0.37)
  waiting for transfers between devices: 358 us -> 0 us
  Pallas kernels: 0 us -> 163 us
  other arithmetic: 38.4 us -> 0 us
  matrix products: 22.5 us -> 0 us
  local copies, waits for them, and re-layouts: 27.9 us -> 12.4 us
  between operations: 13.2 us -> 0.01 us
  starting transfers between devices: 12.9 us -> 0 us
    psum x1 -> x0, waiting for transfers between devices: 219 us -> none  [on_device(): lax.psum(partial_sum.astype(jnp.bfloat16), 'tp').astype(jnp.float32)]
    pallas_call x0 -> x1, Pallas kernels: none -> 163 us  [on_device(): pl.pallas_call(kernel, name='attention_block', out_shape=jax.ShapeDtypeSt...]
    all_gather x2 -> x0, waiting for transfers between devices: 91.7 us -> none  [the longest x1 53.4 us: on_device(): blocks = lax.all_gather(qkv_shards, 'rep', axis=0, tiled=True)]
    all_to_all x2 -> x0, waiting for transfers between devices: 45.7 us -> none  [the longest x1 45.7 us: on_device(): lax.all_to_all(blocks, 'tp', split_axis=0, concat_axis=2, tiled=True)]
    dot_general x3 -> x0, matrix products: 22.5 us -> none  [the longest x1 10.1 us: on_device(): jnp.einsum('tpr,prd->td', head_parts, local_out[0], preferred_element_typ...]
    reduce_sum x4 -> x0, other arithmetic: 13.8 us -> none  [the longest x1 5.72 us: on_device(): mean_out = jnp.mean(summed * summed, axis=1, keepdims=True)]
    all_to_all x2 -> x0, starting transfers between devices: 12.9 us -> none  [the longest x1 6.57 us: on_device(): lax.all_to_all(blocks, 'tp', split_axis=0, concat_axis=2, tiled=True)]
    convert_element_type x1 -> x0, other arithmetic: 10.8 us -> none  [on_device(): (stream + summed * lax.rsqrt(mean_out + EPS) * gain_post).astype(jnp.bflo...]
  transfers between devices with their start and end apart: 5 -> 0, of which waited for: 4 -> 0; matrix products, arithmetic and copies ran while one was open for 6% -> 0% of each run, Pallas kernels for 0% -> 0%
where the time goes in v1:
time: 176 us; the launch traced here: 175 us
  Pallas kernels  163 us (93%)
  local copies, waits for them, and re-layouts  12.4 us (7%)
    pallas_call x1, Pallas kernels, on_device(): pl.pallas_call(kernel, name='attention_block', out_shape=jax.ShapeDtypeSt...  163 us
    unnamed x2, local copies, waits for them, and re-layouts  9.74 us

profile of v1, /device:TPU:1, one launch (start us, length us, event | category | flops | bytes accessed | tf_op | source)
XLA Modules:
  0.0 175.0 jit_solution(6573606536732056210)
XLA Ops:
  0.0 1.3 reshape.9.gpre
  1.3 1.3 reshape.10.gpost
  2.7 1.7 copy.9.outs
  4.4 162.6 %attention_block.1 = bf16[1024,4608]{1,0:T(8,128)(2,1)} custom-call(bf16[1024,4608]{1,0:T(8,128)(2,1)} %tok.1, f32[1,4608]{1,0:T(1,128)} %reshape.9.gpre, f32[1,4608]{1,0:T(1,128)} %reshape.10.gpost, f32[1,128]{1,0:T(1,128)} %constant.2.clone.freq, bf16[1,576,256]{2,1,0:T(8,128)(2,1)} %qkv.1, bf16[1,128,576]{2,1,0:T(8,128)(2,1)} %copy.9.outs, s32[16]{0:T(128)} %smap.1, ...), custom_call_target="tpu_custom_call" | custom-call | flops 25999998976 | bytes 30000000 | tf_op jit(solution)/shard_map/attention_block/pallas_call | solution.py:352
  167.0 8.0 %copy.11 = bf16[1024,4608]{1,0:T(8,128)(2,1)} copy(bf16[1024,4608]{1,0:T(8,128)(2,1)} %attention_block.1) | data formatting | bytes 18874368

commit v2 on v1

v2 whole, which is shorter than its diff:
```python
import math

import jax
import jax.numpy as jnp
import numpy as np
from jax import lax
from jax.experimental import pallas as pl
from jax.experimental.pallas import tpu as pltpu
from jax.sharding import PartitionSpec as P

D = 4608
TOK = 1024
HDIM = 128
CHUNK = 256
N_CHUNK = TOK // CHUNK
SEG = 576
PART = 144
QUERY_SCALE = 1.0 / 12.0
EPS = 1e-06
MESH = pl.DeviceIdType.MESH
F32 = jnp.float32
BF16 = jnp.bfloat16
NT = (((1,), (1,)), ((), ()))
W_N = (256, 192, 128)
W_OFF = ((0, 320), (384, 0), (256, 192))
W_ORDER = ("yzx", "xyz", "zxy")
W_COL = ((0, 896), (384, 576), (256, 768))


def device(x, y, z, c):
    return ((z % 2) * 8 + y * 2 + c, (z // 2) * 4 + x)


def kernel(
    tok, gpre, gpost, freq, qkv, outs, smap, pos, o_ref,
    s1, send2, wq, wa, wb, wc, h0, h1, h2, h3, normed, qb, kv, cosb, sinb, startb, total, gain1, gain2,
    s1_ss, s1_rs, s2_ss, s2_rs, s3_ss, s3_rs, w_ss, w_rs, h_ss, h_rs, loc,
):
    hs = (h0, h1, h2, h3)
    ws = (wa, wb, wc)
    rep = lax.axis_index("rep")
    tp = lax.axis_index("tp")
    c, y, zl = rep % 2, (rep // 2) % 4, rep // 8
    x, zh = tp % 4, tp // 4
    z = zh * 2 + zl
    yp, ym, y2 = (y + 1) % 4, (y + 3) % 4, (y + 2) % 4
    xp, xm, x2 = (x + 1) % 4, (x + 3) % 4, (x + 2) % 4
    full = slice(None)

    def shifted(axis, by):
        at = {"x": x, "y": y, "z": z}
        at[axis] = (at[axis] + by + 4) % 4
        return device(at["x"], at["y"], at["z"], c)

    def remote(src, dst, ss, rs, dev):
        return pltpu.make_async_remote_copy(
            src_ref=src, dst_ref=dst, send_sem=ss, recv_sem=rs, device_id=dev, device_id_type=MESH
        )

    started = []

    def go(cp):
        cp.start()
        started.append(cp)
        return cp

    tok_copies = []
    for i in range(N_CHUNK):
        rows = pl.ds(i * CHUNK, CHUNK)
        cp = pltpu.make_async_copy(tok.at[rows], o_ref.at[rows], loc.at[i])
        cp.start()
        tok_copies.append(cp)
    w_own = []
    for p in range(3):
        off = pl.multiple_of(jnp.where(x % 2 == 0, W_OFF[p][0], W_OFF[p][1]), 64)
        cp = pltpu.make_async_copy(outs.at[0, pl.ds(off, W_N[p])], ws[p].at[z, y, c, x], loc.at[6 + p])
        cp.start()
        w_own.append(cp)

    barrier = pltpu.get_barrier_semaphore()

    def greet_rep(d, _):
        pl.semaphore_signal(barrier, inc=1, device_id=((rep + d) % 16, tp), device_id_type=MESH)
        return 0

    def greet_tp(d, _):
        pl.semaphore_signal(barrier, inc=1, device_id=(rep, (tp + d) % 8), device_id_type=MESH)
        return 0

    lax.fori_loop(1, 16, greet_rep, 0)
    lax.fori_loop(1, 8, greet_tp, 0)
    far = jnp.where(zl == 0, 3, 1)
    pl.semaphore_signal(barrier, inc=1, device_id=device(x, y, (z + far) % 4, c), device_id_type=MESH)
    pl.semaphore_wait(barrier, 23)

    place = rep // 2
    sib = (rep + 1 - 2 * c, tp)

    def s1_src(to):
        rows = pl.ds(pl.multiple_of((to % 4) * PART, 16), PART)
        cols = pl.ds(pl.multiple_of((to // 4) * 128, 128), 128)
        return qkv.at[0, rows, cols]

    own1 = pltpu.make_async_copy(s1_src(place), s1.at[place, c], loc.at[4])
    own1.start()

    def s1_copy(d):
        to = (place + d) % 8
        return remote(s1_src(to), s1.at[place, c], s1_ss.at[d], s1_rs.at[d], (to * 2 + c, tp))

    lax.fori_loop(1, 8, lambda d, _: (s1_copy(d).start(), 0)[1], 0)

    def w_set(p, done, axis=None, by=0, half=None):
        at = {"x": x, "y": y, "z": z}
        if axis is not None:
            at[axis] = (at[axis] + by + 4) % 4
        n = W_N[p]
        rows = pl.ds(0, n) if half is None else pl.ds(half * (n // 2), n // 2)
        iz, iy, ix = (full if a in done else at[a] for a in "zyx")
        return ws[p].at[iz, iy, c, ix, rows]

    w_in = {}

    def w_send(p, step):
        axis, done = W_ORDER[p][step], W_ORDER[p][:step]
        ways = ((1, 0), (-1, 1), (1, 1), (-1, 0)) if step == 2 else ((1, None), (-1, None), (2, None))
        cps = []
        for k, (by, half) in enumerate(ways):
            block = w_set(p, done, half=half)
            cps.append(go(remote(block, block, w_ss.at[p, step, k], w_rs.at[p, step, k], shifted(axis, by))))
        w_in[p, step] = cps

    def w_wait(p, step):
        for cp in w_in[p, step]:
            cp.wait_recv()

    def w_relay(p):
        axis, done = W_ORDER[p][2], W_ORDER[p][:2]
        cps = w_in[p, 2]
        for k, (by, half) in enumerate(((1, 0), (-1, 1))):
            cps[k].wait_recv()
            block = w_set(p, done, axis, -by, half)
            cps.append(go(remote(block, block, w_ss.at[p, 2, 4 + k], w_rs.at[p, 2, 4 + k], shifted(axis, by))))

    w_sib = {0: [], 1: [], 2: []}

    def w_share(p, by):
        axis, done = W_ORDER[p][2], W_ORDER[p][:2]
        k = len(w_sib[p])
        block = w_set(p, done, axis, by)
        w_sib[p].append(go(remote(block, block, w_ss.at[p, 3, k], w_rs.at[p, 3, k], sib)))

    def w_all(p):
        cps = w_in[p, 2]
        for cp in cps[2:4]:
            cp.wait_recv()
        w_share(p, 1)
        w_share(p, -1)
        for cp in cps[4:]:
            cp.wait_recv()
        w_share(p, 2)

    def w_ready(p):
        for cp in w_sib[p]:
            cp.wait_recv()

    for cp in w_own:
        cp.wait()
    for p in range(3):
        w_send(p, 0)

    for k in range(D // 128):
        gain1[:, k * 128:(k + 1) * 128] = gpre[k:k + 1, :]
        gain2[:, k * 128:(k + 1) * 128] = gpost[k:k + 1, :]

    def norm_rows(i, _):
        rows = pl.ds(pl.multiple_of(i * 32, 32), 32)
        v = o_ref[rows, :].astype(F32)
        ms = jnp.sum(v * v, axis=1, keepdims=True) * (1.0 / D)
        normed[rows, :] = (v * lax.rsqrt(ms + EPS) * gain1[...]).astype(BF16)
        return 0

    for cp in tok_copies:
        cp.wait()
    lax.fori_loop(0, 12, norm_rows, 0)
    for p in range(3):
        w_wait(p, 0)
    for p in range(3):
        w_send(p, 1)
    lax.fori_loop(1, 8, lambda d, _: (s1_copy(d).wait_recv(), 0)[1], 0)
    own1.wait()
    swap = go(remote(s1.at[:, c], s1.at[:, c], s1_ss.at[0], s1_rs.at[0], sib))
    lax.fori_loop(12, 20, norm_rows, 0)
    swap.wait_recv()

    def order_of(b):
        at = jnp.int32(0)
        for s in range(16):
            at = jnp.where(smap[s] == b, s, at)
        return at

    for t in range(8):
        at = order_of(2 * t + c)
        send2[t] = s1[at // 2, at % 2]
    g = c * 2 + zl
    g2 = c * 2 + (1 - zl)

    own2 = pltpu.make_async_copy(send2.at[tp], wq.at[g, tp, y], loc.at[5])
    own2.start()

    def s2_copy(d):
        to = (tp + d) % 8
        return remote(send2.at[to], wq.at[g, tp, y], s2_ss.at[d], s2_rs.at[d], (rep, to))

    lax.fori_loop(1, 8, lambda d, _: (s2_copy(d).start(), 0)[1], 0)
    lax.fori_loop(20, 32, norm_rows, 0)

    lax.fori_loop(1, 8, lambda d, _: (s2_copy(d).wait_recv(), 0)[1], 0)
    own2.wait()

    zdev = ((1 - zl) * 8 + y * 2 + c, tp)
    updev, dndev = shifted("y", 1), shifted("y", -1)
    lo, hi = pl.ds(0, 4), pl.ds(4, 4)
    k3 = [0]

    def s3_send(block, dev):
        k = k3[0]
        k3[0] += 1
        return go(remote(block, block, s3_ss.at[k], s3_rs.at[k], dev))

    z_lo = s3_send(wq.at[g, lo, y], zdev)
    up_lo = s3_send(wq.at[g, lo, y], updev)
    dn_hi = s3_send(wq.at[g, hi, y], dndev)
    z_hi = s3_send(wq.at[g, hi, y], zdev)
    up_hi = s3_send(wq.at[g, hi, y], updev)
    dn_lo = s3_send(wq.at[g, lo, y], dndev)
    sib_a = [s3_send(wq.at[g, :, y], sib)]
    sib_b = []
    for p in range(2):
        w_wait(p, 1)
        w_send(p, 2)
        w_share(p, 0)
    pos_t = pos[...].astype(F32).T
    lane = lax.broadcasted_iota(jnp.int32, (128, 128), 1)
    for i in range(8):
        at = pos_t[:, i:i + 1]
        angle = at * freq[...]
        rows = pl.ds(i * 128, 128)
        cosb[rows, :] = jnp.cos(angle)
        sinb[rows, :] = jnp.where(lane < 64, -1.0, 1.0) * jnp.sin(angle)
        row = lax.broadcasted_iota(jnp.int32, (128, 128), 0) + i * 128
        startb[rows, :] = row - at.astype(jnp.int32)
    up_lo.wait_recv()
    r_up = s3_send(wq.at[g, lo, ym], updev)
    dn_hi.wait_recv()
    r_dn = s3_send(wq.at[g, hi, yp], dndev)
    z_lo.wait_recv()
    up_tlo = s3_send(wq.at[g2, lo, y], updev)
    z_hi.wait_recv()
    dn_thi = s3_send(wq.at[g2, hi, y], dndev)
    up_thi = s3_send(wq.at[g2, hi, y], updev)
    dn_tlo = s3_send(wq.at[g2, lo, y], dndev)
    sib_b.append(s3_send(wq.at[g2, :, y], sib))
    up_hi.wait_recv()
    sib_a.append(s3_send(wq.at[g, :, ym], sib))
    dn_lo.wait_recv()
    sib_a.append(s3_send(wq.at[g, :, yp], sib))
    w_relay(0)
    r_up.wait_recv()
    r_dn.wait_recv()
    sib_a.append(s3_send(wq.at[g, :, y2], sib))
    up_tlo.wait_recv()
    r_tup = s3_send(wq.at[g2, lo, ym], updev)
    dn_thi.wait_recv()
    r_tdn = s3_send(wq.at[g2, hi, yp], dndev)
    w_relay(1)
    w_wait(2, 1)
    w_send(2, 2)
    w_share(2, 0)
    for cp in sib_a:
        cp.wait_recv()

    def project(i, which):
        rows = pl.ds(i * CHUNK, CHUNK)
        weights = jnp.concatenate([wq[which].reshape(D, 128), wq[2 + which].reshape(D, 128)], axis=1)
        p = jnp.dot(normed[rows, :], weights, preferred_element_type=F32)
        cos, sin = cosb[rows, :], sinb[rows, :]

        def rotate(u):
            return u * cos + pltpu.roll(u, 64, 1) * sin

        qb[which, rows, :] = (rotate(p[:, :128]) * QUERY_SCALE).astype(BF16)
        u = p[:, 128:]
        kv[which, rows, :] = jnp.where(which == 0, rotate(u), u).astype(BF16)

    project(0, zl)
    up_thi.wait_recv()
    sib_b.append(s3_send(wq.at[g2, :, ym], sib))
    dn_tlo.wait_recv()
    sib_b.append(s3_send(wq.at[g2, :, yp], sib))
    project(1, zl)
    project(2, zl)
    project(3, zl)
    r_tup.wait_recv()
    r_tdn.wait_recv()
    sib_b.append(s3_send(wq.at[g2, :, y2], sib))
    for cp in sib_b:
        cp.wait_recv()

    def attend(i):
        rows = pl.ds(i * CHUNK, CHUNK)
        n = (i + 1) * CHUNK
        first = startb[rows, 0:1]
        at = lax.broadcasted_iota(jnp.int32, (CHUNK, n), 1)
        row = lax.broadcasted_iota(jnp.int32, (CHUNK, n), 0) + i * CHUNK
        allowed = (at <= row) & (at >= first)
        for j in range(2):
            s = lax.dot_general(qb[j, rows, :], kv[0, 0:n, :], NT, preferred_element_type=F32)
            s = jnp.where(allowed, s, -1e30)
            e = jnp.exp(s - jnp.max(s, axis=1, keepdims=True))
            a = (e * (1.0 / jnp.sum(e, axis=1, keepdims=True))).astype(BF16)
            hs[i][zh, x, j] = jnp.dot(a, kv[1, 0:n, :], preferred_element_type=F32).astype(BF16)

    zpair = (rep, (tp + 4) % 8)
    xup, xdn = shifted("x", 1), shifted("x", -1)
    oz = 1 - zh
    top, bot = pl.ds(0, CHUNK // 2), pl.ds(CHUNK // 2, CHUNK // 2)
    h_in = [dict() for _ in range(N_CHUNK)]

    def h_send(i, name, block, dev):
        k = len(h_in[i])
        h_in[i][name] = go(remote(block, block, h_ss.at[i, k], h_rs.at[i, k], dev))

    def h_got(i, name):
        h_in[i][name].wait_recv()

    def h_stage(i, stage):
        h = hs[i]
        if stage == 0:
            h_send(i, "z0", h.at[zh, x, 0], zpair)
            h_send(i, "u1t", h.at[zh, x, 1, top], xup)
            h_send(i, "d1b", h.at[zh, x, 1, bot], xdn)
            h_send(i, "u1b", h.at[zh, x, 1, bot], xup)
            h_send(i, "d1t", h.at[zh, x, 1, top], xdn)
            h_send(i, "u0t", h.at[zh, x, 0, top], xup)
            h_send(i, "d0b", h.at[zh, x, 0, bot], xdn)
            h_send(i, "u0b", h.at[zh, x, 0, bot], xup)
            h_send(i, "d0t", h.at[zh, x, 0, top], xdn)
            h_send(i, "z1", h.at[zh, x, 1], zpair)
        elif stage == 1:
            h_got(i, "u1t")
            h_send(i, "ru1", h.at[zh, xm, 1, top], xup)
            h_got(i, "d1b")
            h_send(i, "rd1", h.at[zh, xp, 1, bot], xdn)
            h_got(i, "z0")
            h_send(i, "v0t", h.at[oz, x, 0, top], xup)
            h_send(i, "e0b", h.at[oz, x, 0, bot], xdn)
            h_send(i, "v0b", h.at[oz, x, 0, bot], xup)
            h_send(i, "e0t", h.at[oz, x, 0, top], xdn)
            h_got(i, "u1b")
            h_send(i, "zm", h.at[zh, xm, 1], zpair)
            h_got(i, "d1t")
            h_send(i, "zp", h.at[zh, xp, 1], zpair)
        elif stage == 2:
            h_got(i, "u0t")
            h_send(i, "ru0", h.at[zh, xm, 0, top], xup)
            h_got(i, "d0b")
            h_send(i, "rd0", h.at[zh, xp, 0, bot], xdn)
            h_got(i, "ru1")
            h_got(i, "rd1")
            h_send(i, "z2", h.at[zh, x2, 1], zpair)
            h_got(i, "v0t")
            h_send(i, "rv0", h.at[oz, xm, 0, top], xup)
            h_got(i, "e0b")
            h_send(i, "re0", h.at[oz, xp, 0, bot], xdn)
        else:
            for name in ("u0b", "d0t", "v0b", "e0t", "z1", "zm", "zp", "z2", "ru0", "rd0", "rv0", "re0"):
                h_got(i, name)

    def heads_of(i):
        project(i, 1 - zl)
        attend(i)
        h_stage(i, 0)

    heads_of(0)
    heads_of(1)
    w_relay(2)
    h_stage(0, 1)
    heads_of(2)
    w_all(0)
    h_stage(0, 2)
    h_stage(1, 1)
    project(3, 1 - zl)
    attend(3)
    w_all(1)
    h_stage(0, 3)
    h_stage(1, 2)
    h_stage(2, 1)
    h_stage(3, 0)

    def out_proj(p, i):
        rows = pl.ds(i * CHUNK, CHUNK)
        n = W_N[p]
        left = []
        for s in range(16):
            b = smap[s]
            left.append(hs[i][b // 8, (b // 2) % 4, b % 2])
        left = jnp.concatenate(left, axis=1)
        squares = jnp.zeros((CHUNK, 1), F32)
        for half in range(2):
            right = jnp.concatenate(
                [ws[p][half * 2 + r // 8, (r // 2) % 4, r % 2].reshape(4 * n, 128) for r in range(16)], axis=1
            )
            t = lax.dot_general(left, right, NT, preferred_element_type=F32)
            squares = squares + jnp.sum(t * t, axis=1, keepdims=True)
            t = t.astype(BF16)
            for pair in range(2):
                col = half * 2304 + pair * 1152
                a, b = t[:, 2 * pair * n:(2 * pair + 1) * n], t[:, (2 * pair + 1) * n:(2 * pair + 2) * n]
                if p == 1:
                    normed[rows, col + 384:col + 768] = t[:, 2 * pair * n:(2 * pair + 2) * n]
                else:
                    normed[rows, col + W_COL[p][0]:col + W_COL[p][0] + n] = a
                    normed[rows, col + W_COL[p][1]:col + W_COL[p][1] + n] = b
        squares = jnp.broadcast_to(squares, (CHUNK, 128))
        total[rows, :] = squares if p == 0 else total[rows, :] + squares

    def finish(i):
        rows = pl.ds(i * CHUNK, CHUNK)
        scale = lax.rsqrt(total[rows, 0:1] * (1.0 / D) + EPS)
        o_ref[rows, :] = (
            o_ref[rows, :].astype(F32) + normed[rows, :].astype(F32) * scale * gain2[...]
        ).astype(BF16)

    w_ready(0)
    out_proj(0, 0)
    h_stage(1, 3)
    h_stage(2, 2)
    w_ready(1)
    out_proj(1, 0)
    h_stage(3, 1)
    out_proj(0, 1)
    out_proj(1, 1)
    w_all(2)
    h_stage(2, 3)
    w_ready(2)
    out_proj(2, 0)
    finish(0)
    h_stage(3, 2)
    out_proj(2, 1)
    finish(1)
    for p in range(3):
        out_proj(p, 2)
    finish(2)
    h_stage(3, 3)
    for p in range(3):
        out_proj(p, 3)
    finish(3)

    lax.fori_loop(1, 8, lambda d, _: (s1_copy(d).wait_send(), 0)[1], 0)
    lax.fori_loop(1, 8, lambda d, _: (s2_copy(d).wait_send(), 0)[1], 0)
    for cp in started:
        cp.wait_send()


def on_device(tokens, gain_pre, gain_post, qkv_shards, out_shards, shard_map, positions):
    freq = np.exp(np.arange(64) * (-2.0 * math.log(10000.0) / HDIM)).astype(np.float32)
    freq = jnp.asarray(np.concatenate([freq, freq])[None])
    vmem, hbm = pl.BlockSpec(memory_space=pltpu.VMEM), pl.BlockSpec(memory_space=pl.ANY)
    smem = pl.BlockSpec(memory_space=pltpu.SMEM)
    sem = pltpu.SemaphoreType.DMA
    heads = pltpu.VMEM((2, 4, 2, CHUNK, 128), BF16)
    return pl.pallas_call(
        kernel,
        name="attention_block",
        out_shape=pltpu.VMEM((TOK, D), BF16),
        in_specs=[hbm, vmem, vmem, vmem, hbm, hbm, smem, vmem],
        out_specs=vmem,
        scratch_shapes=[
            pltpu.VMEM((8, 2, PART, 128), BF16),
            pltpu.VMEM((8, PART, 128), BF16),
            pltpu.VMEM((4, 8, 4, PART, 128), BF16),
            *[pltpu.VMEM((4, 4, 2, 4, n, 128), BF16) for n in W_N],
            heads, heads, heads, heads,
            pltpu.VMEM((TOK, D), BF16),
            pltpu.VMEM((2, TOK, 128), BF16),
            pltpu.VMEM((2, TOK, 128), BF16),
            pltpu.VMEM((TOK, 128), F32),
            pltpu.VMEM((TOK, 128), F32),
            pltpu.VMEM((TOK, 128), jnp.int32),
            pltpu.VMEM((TOK, 128), F32),
            pltpu.VMEM((1, D), F32),
            pltpu.VMEM((1, D), F32),
            sem((8,)), sem((8,)), sem((8,)), sem((8,)), sem((32,)), sem((32,)),
            sem((3, 4, 6)), sem((3, 4, 6)), sem((4, 24)), sem((4, 24)), sem((12,)),
        ],
        compiler_params=pltpu.CompilerParams(
            collective_id=0, has_side_effects=True, vmem_limit_bytes=52 << 20
        ),
        cost_estimate=pl.CostEstimate(flops=26 * 10**9, bytes_accessed=30 * 10**6, transcendentals=3 * 10**6),
    )(
        tokens, gain_pre.reshape(D // 128, 128), gain_post.reshape(D // 128, 128), freq, qkv_shards, jnp.swapaxes(out_shards, 1, 2),
        shard_map, positions.reshape(8, 128),
    )


def solution(mesh):
    placed = (P("rep", None), P(), P(), P("rep", "tp", None), P("rep", None, "tp"), P(), P("rep"))
    return jax.shard_map(
        on_device, mesh=mesh, in_specs=placed, out_specs=P("rep", None), check_vma=False
    )
```

time: 176 us -> 123 us (0.70)
  Pallas kernels: 163 us -> 120 us
  local copies, waits for them, and re-layouts: 12.4 us -> 3.74 us
    pallas_call x1, Pallas kernels: 163 us -> 120 us  [on_device(): pl.pallas_call(kernel, name='attention_block', out_shape=pltpu.VMEM((TOK,...]
    unnamed x2 -> x1, local copies, waits for them, and re-layouts: 9.74 us -> 3.74 us
    reshape x2 -> x0, local copies, waits for them, and re-layouts: 2.67 us -> none  [the longest x1 1.34 us: on_device(): gain_post.reshape(1, D)]
where the time goes in v2:
time: 123 us
  Pallas kernels  120 us (98%)
  local copies, waits for them, and re-layouts  3.74 us (3%)
    pallas_call x1, Pallas kernels, on_device(): pl.pallas_call(kernel, name='attention_block', out_shape=pltpu.VMEM((TOK,...  120 us
    unnamed x1, local copies, waits for them, and re-layouts  3.74 us

profile of v2, /device:TPU:1, one launch (start us, length us, event | category | flops | bytes accessed | tf_op | source)
XLA Modules:
  0.0 123.3 jit_solution(9603346238277354226)
XLA Ops:
  0.0 119.5 %attention_block.1 = bf16[1024,4608]{1,0:T(8,128)(2,1)S(1)} custom-call(bf16[1024,4608]{1,0:T(8,128)(2,1)} %tok.1, f32[36,128]{1,0:T(8,128)} %bitcast.5, f32[36,128]{1,0:T(8,128)} %bitcast.6, f32[1,128]{1,0:T(1,128)} %constant.2.clone.freq, bf16[1,576,256]{2,1,0:T(8,128)(2,1)} %qkv.1, bf16[1,576,128]{2,1,0:T(8,128)(2,1)} %bitcast.4, s32[16]{0:T(128)} %smap.1, ...), custom_call_target="tpu_custom_call" | custom-call | flops 25999998976 | bytes 30000000 | tf_op jit(solution)/shard_map/attention_block/pallas_call | solution.py:473
  119.5 3.7 %copy.10 = bf16[1024,4608]{1,0:T(8,128)(2,1)} copy(bf16[1024,4608]{1,0:T(8,128)(2,1)S(1)} %attention_block.1) | data formatting | bytes 18874368
